TPU v7x, 256 devices: a whole 4x4x8 slice. The times are simulated.
256 devices in a mesh: row: 16 (over z_hi, y), col: 16 (over z_lo, x, core).
Axes of the slice: x: 4, y: 4, z: 8 (z_hi: 4, z_lo: 2; z = z_hi * 2 + z_lo), core: 2. Of those that a mesh axis runs over, the one named last changes fastest.
Arguments:
- hidden_act: bfloat16 [768, 26624], P('col', 'row'), may hold values from -6 to 6
- out_grad: bfloat16 [768, 16384], P('row', 'col'), may hold values from -6 to 6
- down_weight: bfloat16 [26624, 16384], P('row', 'col'), may hold values from -0.046875 to 0.046875
Outputs:
- fisher: float32 [26624, 16384], P('row', 'col')
- hidden_grad: bfloat16 [768, 26624], P('col', 'row')
All inputs are finite; a program needn't handle non-finite values.
Results may differ from a plain program's by a relative error of at most 0.001.
Values may be sent and summed in bfloat16 or wider, within the bound.
A program may use at most 64 MiB of HBM per device.

v0:
```python
import jax
import jax.numpy as jnp
from jax import lax
from jax.sharding import PartitionSpec as P

SEQ = 96
EXAMPLES = 8


def per_device(hidden_act, out_grad, down_weight):
    act_whole = lax.all_gather(hidden_act, "col", axis=0, tiled=True)
    grad_whole = lax.all_gather(out_grad, "row", axis=0, tiled=True)
    feat_rows = down_weight.shape[0]
    feat_cols = down_weight.shape[1]

    def accumulate(example, total):
        start = (example * SEQ).astype(jnp.int32)
        act_piece = lax.dynamic_slice_in_dim(act_whole, start, SEQ, 0)
        grad_piece = lax.dynamic_slice_in_dim(grad_whole, start, SEQ, 0)
        grad_e = lax.dot_general(
            act_piece, grad_piece, (((0,), (0,)), ((), ())), preferred_element_type=jnp.float32
        )
        return total + grad_e * grad_e

    total = lax.fori_loop(0, EXAMPLES, accumulate, jnp.zeros((feat_rows, feat_cols), jnp.float32))
    fisher = total / (EXAMPLES * SEQ)
    token_rows = hidden_act.shape[0]
    partial_value = lax.dot_general(
        grad_whole, down_weight, (((1,), (1,)), ((), ())), preferred_element_type=jnp.float32
    )
    whole_sum = lax.psum(partial_value, "col")
    offset = lax.axis_index("col") * token_rows
    summed = lax.dynamic_slice_in_dim(whole_sum, offset, token_rows, 0)
    return (fisher, summed.astype(jnp.bfloat16))


def solution(mesh):
    placed = (P("col", "row"), P("row", "col"), P("row", "col"))
    return jax.shard_map(
        per_device,
        mesh=mesh,
        in_specs=placed,
        out_specs=(P("row", "col"), P("col", "row")),
        check_vma=False,
    )
```

profile of v0, /device:TPU:31, one launch (start us, length us, event | category | flops | bytes accessed | tf_op | source)
XLA Modules:
  0.0 235.9 jit_solution(5703237973999043682)
XLA Ops:
  7.2 0.0 copy-start
  7.2 0.0 all-gather.5.cloned.1.call-start
  7.2 0.7 all-gather.5.cloned.1.call-update
  7.9 0.0 all-gather.3.cloned.1.call-start
  8.0 0.7 all-gather.3.cloned.1.call-update
  8.7 58.4 %all-gather.5.cloned.1.call-done = bf16[768,1024]{1,0:T(8,128)(2,1)} async-done(((bf16[48,1024]{1,0:T(8,128)(2,1)}), bf16[768,1024]{1,0:T(8,128)(2,1)}) %all-gather.5.cloned.1.call-update) | async-done | bytes 1572880 | tf_op jit(solution)/shard_map/all_gather | solution.py:12
  67.0 0.0 copy-done
  67.0 6.7 %fusion.3 = f32[768,1664]{1,0:T(8,128)} fusion(bf16[768,1024]{1,0:T(8,128)(2,1)} %all-gather.5.cloned.1.call-done, bf16[1664,1024]{1,0:T(8,128)(2,1)S(1)} %copy-done), kind=kOutput, calls=%fused_computation.6 | convolution fusion | flops 2617245696 | bytes 10092544 | tf_op jit(solution)/shard_map/dot_general | solution.py:28
  73.7 91.5 %all-reduce.1 = bf16[768,1664]{1,0:T(8,128)(2,1)} all-reduce(f32[768,1664]{1,0:T(8,128)} %fusion.3), channel_id=1, replica_groups=mesh['row'=16,'col'=16] {'col'}, use_global_device_ids=true, to_apply=%region_2.0 | all-reduce | flops 1277952 | bytes 7667712 | tf_op jit(solution)/shard_map/psum | solution.py:31
  165.3 1.6 dynamic-slice_convert_fusion
  166.9 0.0 all-gather.3.cloned.1.call-done
  166.9 54.8 %while.14 = (s32[]{:T(128)}, f32[1664,1024]{1,0:T(8,128)}, bf16[768,1664]{1,0:T(8,128)(2,1)}, bf16[768,1024]{1,0:T(8,128)(2,1)}, s32[]{:T(128)}, /*index=5*/s32[]{:T(128)}, s32[]{:T(128)}, s32[]{:T(128)}) while((s32[]{:T(128)}, f32[1664,1024]{1,0:T(8,128)}, bf16[768,1664]{1,0:T(8,128)(2,1)}, bf16[768,1024]{1,0:T(8,128)(2,1)}, ...), condition=%wide.region_1.0_spmd.clone, body=%wide.region_0.0_spmd.clone.sunk | while | flops 332267520 | bytes 14149268 | solution.py:25
  166.9 5.0 %select_add_fusion.2 = f32[1664,1024]{1,0:T(8,128)} fusion(f32[1664,1024]{1,0:T(8,128)} %get-tuple-element.139, pred[]{:T(512)S(6)} %compare.3, bf16[768,1664]{1,0:T(8,128)(2,1)} %get-tuple-element.148, s32[]{:T(128)S(6)} %select_n.14, bf16[768,1024]{1,0:T(8,128)(2,1)} %get-tuple-element.149), kind=kOutput, calls=%fused_computation.clone.1 | convolution fusion | flops 332267520 | bytes 14149120 | tf_op jit(solution)/shard_map/while/body/eval_jaxpr/dot_general | solution.py:20
  171.9 7.1 %select_add_fusion.2 = f32[1664,1024]{1,0:T(8,128)} fusion(f32[1664,1024]{1,0:T(8,128)} %get-tuple-element.139, pred[]{:T(512)S(6)} %compare.3, bf16[768,1664]{1,0:T(8,128)(2,1)} %get-tuple-element.148, s32[]{:T(128)S(6)} %select_n.14, bf16[768,1024]{1,0:T(8,128)(2,1)} %get-tuple-element.149), kind=kOutput, calls=%fused_computation.clone.1 | convolution fusion | flops 332267520 | bytes 14149120 | tf_op jit(solution)/shard_map/while/body/eval_jaxpr/dot_general | solution.py:20
  179.0 7.1 %select_add_fusion.2 = f32[1664,1024]{1,0:T(8,128)} fusion(f32[1664,1024]{1,0:T(8,128)} %get-tuple-element.139, pred[]{:T(512)S(6)} %compare.3, bf16[768,1664]{1,0:T(8,128)(2,1)} %get-tuple-element.148, s32[]{:T(128)S(6)} %select_n.14, bf16[768,1024]{1,0:T(8,128)(2,1)} %get-tuple-element.149), kind=kOutput, calls=%fused_computation.clone.1 | convolution fusion | flops 332267520 | bytes 14149120 | tf_op jit(solution)/shard_map/while/body/eval_jaxpr/dot_general | solution.py:20
  186.1 7.1 %select_add_fusion.2 = f32[1664,1024]{1,0:T(8,128)} fusion(f32[1664,1024]{1,0:T(8,128)} %get-tuple-element.139, pred[]{:T(512)S(6)} %compare.3, bf16[768,1664]{1,0:T(8,128)(2,1)} %get-tuple-element.148, s32[]{:T(128)S(6)} %select_n.14, bf16[768,1024]{1,0:T(8,128)(2,1)} %get-tuple-element.149), kind=kOutput, calls=%fused_computation.clone.1 | convolution fusion | flops 332267520 | bytes 14149120 | tf_op jit(solution)/shard_map/while/body/eval_jaxpr/dot_general | solution.py:20
  193.2 7.1 %select_add_fusion.2 = f32[1664,1024]{1,0:T(8,128)} fusion(f32[1664,1024]{1,0:T(8,128)} %get-tuple-element.139, pred[]{:T(512)S(6)} %compare.3, bf16[768,1664]{1,0:T(8,128)(2,1)} %get-tuple-element.148, s32[]{:T(128)S(6)} %select_n.14, bf16[768,1024]{1,0:T(8,128)(2,1)} %get-tuple-element.149), kind=kOutput, calls=%fused_computation.clone.1 | convolution fusion | flops 332267520 | bytes 14149120 | tf_op jit(solution)/shard_map/while/body/eval_jaxpr/dot_general | solution.py:20
  200.3 7.1 %select_add_fusion.2 = f32[1664,1024]{1,0:T(8,128)} fusion(f32[1664,1024]{1,0:T(8,128)} %get-tuple-element.139, pred[]{:T(512)S(6)} %compare.3, bf16[768,1664]{1,0:T(8,128)(2,1)} %get-tuple-element.148, s32[]{:T(128)S(6)} %select_n.14, bf16[768,1024]{1,0:T(8,128)(2,1)} %get-tuple-element.149), kind=kOutput, calls=%fused_computation.clone.1 | convolution fusion | flops 332267520 | bytes 14149120 | tf_op jit(solution)/shard_map/while/body/eval_jaxpr/dot_general | solution.py:20
  207.4 7.1 %select_add_fusion.2 = f32[1664,1024]{1,0:T(8,128)} fusion(f32[1664,1024]{1,0:T(8,128)} %get-tuple-element.139, pred[]{:T(512)S(6)} %compare.3, bf16[768,1664]{1,0:T(8,128)(2,1)} %get-tuple-element.148, s32[]{:T(128)S(6)} %select_n.14, bf16[768,1024]{1,0:T(8,128)(2,1)} %get-tuple-element.149), kind=kOutput, calls=%fused_computation.clone.1 | convolution fusion | flops 332267520 | bytes 14149120 | tf_op jit(solution)/shard_map/while/body/eval_jaxpr/dot_general | solution.py:20
  214.6 7.1 %select_add_fusion.2 = f32[1664,1024]{1,0:T(8,128)} fusion(f32[1664,1024]{1,0:T(8,128)} %get-tuple-element.139, pred[]{:T(512)S(6)} %compare.3, bf16[768,1664]{1,0:T(8,128)(2,1)} %get-tuple-element.148, s32[]{:T(128)S(6)} %select_n.14, bf16[768,1024]{1,0:T(8,128)(2,1)} %get-tuple-element.149), kind=kOutput, calls=%fused_computation.clone.1 | convolution fusion | flops 332267520 | bytes 14149120 | tf_op jit(solution)/shard_map/while/body/eval_jaxpr/dot_general | solution.py:20
  221.7 7.4 %broadcast_multiply_fusion = f32[1664,1024]{1,0:T(8,128)} fusion(f32[1664,1024]{1,0:T(8,128)} %get-tuple-element.81), kind=kLoop, calls=%fused_computation.4 | loop fusion | flops 1703936 | bytes 13631488 | tf_op jit(solution)/shard_map/div | solution.py:26
  (1 shorter events, 0.0 us)
Async XLA Ops:
  7.2 59.9 %copy-start = (bf16[1664,1024]{1,0:T(8,128)(2,1)S(1)}, bf16[1664,1024]{1,0:T(8,128)(2,1)}, u32[]{:S(2)}) copy-start(bf16[1664,1024]{1,0:T(8,128)(2,1)} %param.7) | copy-start | bytes 10223620
  7.2 59.8 %all-gather.5.cloned.1.call-start = ((), (), s32[]{:S(2)}) async-start(), calls=%async_computation.1 | async-start | bytes 1671168 | tf_op jit(solution)/shard_map/all_gather | solution.py:12
  7.9 159.0 %all-gather.3.cloned.1.call-start = ((), (), s32[]{:S(2)}) async-start(), calls=%async_computation | async-start | bytes 2715648 | tf_op jit(solution)/shard_map/all_gather | solution.py:11
Sparse Core Ops, SparseCore 0:
  10.4 56.5 all-gather.4
  68.9 39.2 all-gather.2
where the time goes:
time: 238 us; the launch traced here: 236 us
  blocking collectives  91.5 us (38%)
  matrix products  61.5 us (26%)
  waiting for transfers between devices  59.7 us (25%)
  between operations  14.1 us (6%)
  other arithmetic  7.41 us (3%)
    psum x1, blocking collectives, per_device(): whole_sum = lax.psum(partial_value, 'col')  91.5 us
    all_gather x1, waiting for transfers between devices, per_device(): grad_whole = lax.all_gather(out_grad, 'row', axis=0, tiled=True)  58.4 us
    dot_general x8, matrix products, accumulate(): lax.dot_general(act_piece, grad_piece, (((0,), (0,)), ((), ())), preferre...  54.8 us
    div x1, other arithmetic, per_device(): fisher = total / (EXAMPLES * SEQ)  7.4 us
    dot_general x1, matrix products, per_device(): lax.dot_general(grad_whole, down_weight, (((1,), (1,)), ((), ())), prefer...  6.72 us
  transfers between devices with their start and end apart: 2, of which 1 were waited for; matrix products, arithmetic and copies ran while one was open for 4% of the time, Pallas kernels for 0%

commit v1 on v0

v1 whole, which is shorter than its diff:
```python
import jax
import jax.numpy as jnp
from jax import lax
from jax.experimental import pallas as pl
from jax.experimental.pallas import tpu as pltpu
from jax.sharding import PartitionSpec as P

SEQ = 96
EXAMPLES = 8
MESH = pl.DeviceIdType.MESH

TOK = 48
HID = 1664
FEAT = 1024
TOKENS = 768

KINDS = []


def kind(name):
    if name not in KINDS:
        KINDS.append(name)
    return KINDS.index(name)


for j in range(3):
    kind(("gz", j))
for j in range(4):
    for name in ("gyp", "gym", "gyf"):
        kind((name, j))
for j in range(8):
    kind(("gc", j))
for name in ("az", "axp0", "axm0", "axp1", "axm1", "axf0", "axf1"):
    kind(name)
for j in range(8):
    kind(("ac", j))
kind("w")


def kernel(act, grad, weight, fisher, hidden, act_all, grad_all, grad_mate, w_all, left, part, recv,
           send_sems, recv_sems, part_send, part_recv, local_sems):
    r, c = lax.axis_index("row"), lax.axis_index("col")
    zh, y = r // 4, r % 4
    zl, x, core = c // 8, (c // 2) % 4, c % 2
    chip = c // 2

    def row_at(dzh, dy):
        return ((zh + dzh) % 4) * 4 + (y + dy) % 4

    def col_at(dzl, dx, dcore):
        return ((zl + dzl) % 2) * 8 + ((x + dx) % 4) * 2 + (core + dcore) % 2

    mate = (r, col_at(0, 0, 1))

    barrier = pltpu.get_barrier_semaphore()
    peers = [(row_at(dzh, 0), c) for dzh in (1, 2, 3)] + [(row_at(0, dy), c) for dy in (1, 3)]
    peers += [(r, col_at(dzl, dx, dc)) for dzl in range(2) for dx in range(4) for dc in range(2) if (dzl, dx, dc) != (0, 0, 0)]
    for peer in peers:
        pl.semaphore_signal(barrier, inc=1, device_id=peer, device_id_type=MESH)

    def rows(b):
        return pl.ds(pl.multiple_of(b * TOK, TOK), TOK)

    local = [
        pltpu.make_async_copy(grad, grad_all.at[rows(r)], local_sems.at[0]),
        pltpu.make_async_copy(act, act_all.at[rows(c)], local_sems.at[1]),
        pltpu.make_async_copy(weight, w_all.at[:, pl.ds(0, FEAT)], local_sems.at[2]),
    ]
    for copy in local:
        copy.start()
    pl.semaphore_wait(barrier, len(peers))

    sent = []

    def send(name, src, dst, to):
        k = kind(name)
        copy = pltpu.make_async_remote_copy(
            src_ref=src, dst_ref=dst, send_sem=send_sems.at[k], recv_sem=recv_sems.at[k],
            device_id=to, device_id_type=MESH,
        )
        copy.start()
        sent.append((name, copy))

    def arrived(name):
        for n, copy in sent:
            if n == name:
                copy.wait_recv()
                return
        raise ValueError(name)

    def send_grad(name, b, to, src=None):
        send(name, grad_all.at[rows(b)] if src is None else src, grad_all.at[rows(b)], to)

    def send_act(name, b, to, src=None):
        send(name, act_all.at[rows(b)] if src is None else src, act_all.at[rows(b)], to)

    zstep = (0, -1, 1, 2)

    def to_mate(first, y_block):
        for i in range(2):
            b = ((1 - core) + 2 * i) * 4 + y_block
            send(("gc", first + i), grad_all.at[rows(b)], grad_mate.at[rows(b)], mate)

    send_grad(("gz", 0), r, (row_at(1, 0), c), grad)
    send_grad(("gz", 1), r, (row_at(-1, 0), c), grad)
    send_grad(("gz", 2), r, (row_at(2, 0), c), grad)
    send_grad(("gyp", 0), r, (row_at(0, 1), c), grad)
    send_grad(("gym", 0), r, (row_at(0, -1), c), grad)
    send_act("az", c, (r, col_at(1, 0, 0)), act)
    send_act("axp0", c, (r, col_at(0, 1, 0)), act)
    send_act("axm0", c, (r, col_at(0, -1, 0)), act)
    send("w", weight, w_all.at[:, pl.ds(FEAT, FEAT)], mate)
    send_act(("ac", 0), c, mate, act)

    for j in (1, 2):
        arrived(("gz", j - 1))
        b = row_at(zstep[j], 0)
        send_grad(("gyp", j), b, (row_at(0, 1), c))
        send_grad(("gym", j), b, (row_at(0, -1), c))
    arrived("az")
    b = col_at(1, 0, 0)
    send_act("axp1", b, (r, col_at(0, 1, 0)))
    send_act("axm1", b, (r, col_at(0, -1, 0)))
    send_act(("ac", 1), b, mate)
    arrived(("gz", 2))
    b = row_at(2, 0)
    send_grad(("gyp", 3), b, (row_at(0, 1), c))
    send_grad(("gym", 3), b, (row_at(0, -1), c))
    for copy in local:
        copy.wait()
    to_mate(0, y)

    def forward_y(j):
        if j < 2:
            arrived(("gyp", j))
            send_grad(("gyf", j), row_at(zstep[j], -1), (row_at(0, 1), c))
        else:
            arrived(("gym", j))
            send_grad(("gyf", j), row_at(zstep[j], 1), (row_at(0, -1), c))

    forward_y(0)
    forward_y(1)
    forward_y(2)

    arrived("axp0")
    b = col_at(0, -1, 0)
    send_act("axf0", b, (r, col_at(0, 1, 0)))
    send_act(("ac", 2), b, mate)
    arrived("axm0")
    send_act(("ac", 3), col_at(0, 1, 0), mate)

    def multiply(first, y_blocks):
        blocks = [(core + 2 * i) * 4 + yb for yb in y_blocks for i in range(2)]
        count = len(blocks)
        for i, b in enumerate(blocks):
            left[pl.ds(i * TOK, TOK), pl.ds(0, FEAT)] = grad_all[rows(b), :]
            left[pl.ds(i * TOK, TOK), pl.ds(FEAT, FEAT)] = grad_mate[rows(b), :]

        def tile(start, width):
            value = lax.dot_general(
                left[pl.ds(0, count * TOK), :], w_all[pl.ds(start, width), :],
                (((1,), (1,)), ((), ())), preferred_element_type=jnp.float32,
            )
            for i in range(count):
                part[first + i, :, pl.ds(start, width)] = value[i * TOK:(i + 1) * TOK]

        @pl.loop(0, HID // 256)
        def _(n):
            tile(pl.multiple_of(n * 256, 256), 256)

        tile(HID // 256 * 256, HID % 256)
        for i, b in enumerate(blocks):
            @pl.when(b == c)
            def _():
                copy = pltpu.make_async_copy(part.at[first + i], recv.at[chip], part_recv.at[chip])
                copy.start()

            @pl.when(b != c)
            def _():
                pltpu.make_async_remote_copy(
                    src_ref=part.at[first + i], dst_ref=recv.at[chip], send_sem=part_send.at[first + i],
                    recv_sem=part_recv.at[chip], device_id=(r, b), device_id_type=MESH,
                ).start()
        return blocks

    arrived("w")
    arrived(("gc", 0))
    arrived(("gc", 1))
    dests = multiply(0, [y])

    forward_y(3)
    arrived("axm1")
    b = col_at(1, 1, 0)
    send_act("axf1", b, (r, col_at(0, -1, 0)))
    send_act(("ac", 4), b, mate)
    arrived("axp1")
    send_act(("ac", 5), col_at(1, -1, 0), mate)
    for j in (2, 3):
        arrived(("gyp", j))
    to_mate(2, (y - 1) % 4)
    for j in (0, 1):
        arrived(("gym", j))
    to_mate(4, (y + 1) % 4)
    for j in range(2, 6):
        arrived(("gc", j))
    dests += multiply(2, [(y - 1) % 4, (y + 1) % 4])

    for j in range(4):
        arrived(("gyf", j))
    to_mate(6, (y + 2) % 4)
    arrived("axf0")
    send_act(("ac", 6), col_at(0, 2, 0), mate)
    arrived("axf1")
    send_act(("ac", 7), col_at(1, 2, 0), mate)
    for j in range(6, 8):
        arrived(("gc", j))
    dests += multiply(6, [(y + 2) % 4])

    for j in range(8):
        arrived(("ac", j))

    @pl.loop(0, HID // 128)
    def _(n):
        start = pl.multiple_of(n * 128, 128)
        for f in range(FEAT // 256):
            total = jnp.zeros((128, 256), jnp.float32)
            for e in range(EXAMPLES):
                piece = lax.dot_general(
                    act_all[pl.ds(e * SEQ, SEQ), pl.ds(start, 128)], grad_all[pl.ds(e * SEQ, SEQ), pl.ds(f * 256, 256)],
                    (((0,), (0,)), ((), ())), preferred_element_type=jnp.float32,
                )
                total = total + piece * piece
            fisher[pl.ds(start, 128), pl.ds(f * 256, 256)] = total / (EXAMPLES * SEQ)

    for k in range(8):
        pltpu.make_async_copy(part.at[0], recv.at[k], part_recv.at[k]).wait()

    @pl.loop(0, TOK // 16)
    def _(n):
        at = pl.ds(pl.multiple_of(n * 16, 16), 16)
        total = recv[0, at, :]
        for k in range(1, 8):
            total = total + recv[k, at, :]
        hidden[at, :] = total.astype(jnp.bfloat16)

    for _, copy in sent:
        copy.wait_send()
    for i, b in enumerate(dests):
        @pl.when(b != c)
        def _():
            pltpu.make_async_remote_copy(
                src_ref=part.at[i], dst_ref=recv.at[chip], send_sem=part_send.at[i],
                recv_sem=part_recv.at[chip], device_id=(r, b), device_id_type=MESH,
            ).wait_send()


def per_device(hidden_act, out_grad, down_weight):
    any_spec = pl.BlockSpec(memory_space=pl.ANY)
    return pl.pallas_call(
        kernel,
        out_shape=(
            pltpu.VMEM((HID, FEAT), jnp.float32),
            jax.ShapeDtypeStruct((TOK, HID), jnp.bfloat16),
        ),
        in_specs=[any_spec] * 3,
        out_specs=(pl.BlockSpec(memory_space=pltpu.VMEM), pl.BlockSpec(memory_space=pltpu.VMEM)),
        scratch_shapes=[
            pltpu.VMEM((TOKENS, HID), jnp.bfloat16),
            pltpu.VMEM((TOKENS, FEAT), jnp.bfloat16),
            pltpu.VMEM((TOKENS, FEAT), jnp.bfloat16),
            pltpu.VMEM((HID, 2 * FEAT), jnp.bfloat16),
            pltpu.VMEM((4 * TOK, 2 * FEAT), jnp.bfloat16),
            pltpu.VMEM((8, TOK, HID), jnp.float32),
            pltpu.VMEM((8, TOK, HID), jnp.float32),
            pltpu.SemaphoreType.DMA((len(KINDS),)),
            pltpu.SemaphoreType.DMA((len(KINDS),)),
            pltpu.SemaphoreType.DMA((8,)),
            pltpu.SemaphoreType.DMA((8,)),
            pltpu.SemaphoreType.DMA((3,)),
        ],
        compiler_params=pltpu.CompilerParams(
            collective_id=0, has_side_effects=True, vmem_limit_bytes=36 * 1024 * 1024,
        ),
        name="fused_grads",
    )(hidden_act, out_grad, down_weight)


def solution(mesh):
    placed = (P("col", "row"), P("row", "col"), P("row", "col"))
    return jax.shard_map(
        per_device,
        mesh=mesh,
        in_specs=placed,
        out_specs=(P("row", "col"), P("col", "row")),
        check_vma=False,
    )
```

time: 238 us -> 78 us (0.33)
  the two profiles are of different devices: /device:TPU:31 before, /device:TPU:8 now
where the time goes in v1:
time: 78 us; the launch traced here: 77.8 us
  Pallas kernels  69.9 us (90%)
  local copies, waits for them, and re-layouts  7.3 us (9%)
    pallas_call x1, Pallas kernels, per_device(): pl.pallas_call(kernel, out_shape=(pltpu.VMEM((HID, FEAT), jnp.float32), j...  69.9 us
    unnamed x8, local copies, waits for them, and re-layouts  7.3 us

profile of v1, /device:TPU:8, one launch (start us, length us, event | category | flops | bytes accessed | tf_op | source)
XLA Modules:
  0.0 77.8 jit_solution(18117831059686314646)
XLA Ops:
  0.6 0.0 copy-start
  0.6 2.0 %copy-done = bf16[1664,1024]{1,0:T(8,128)(2,1)S(1)} copy-done((bf16[1664,1024]{1,0:T(8,128)(2,1)S(1)}, bf16[1664,1024]{1,0:T(8,128)(2,1)}, u32[]{:S(2)}) %copy-start) | copy-done | bytes 3407896
  2.6 0.0 copy-start.1
  2.6 0.9 %copy-done.1 = bf16[48,1664]{1,0:T(8,128)(2,1)S(1)} copy-done((bf16[48,1664]{1,0:T(8,128)(2,1)S(1)}, bf16[48,1664]{1,0:T(8,128)(2,1)}, u32[]{:S(2)}) %copy-start.1) | copy-done | bytes 159768
  3.5 0.0 copy-start.2
  3.5 0.9 %copy-done.2 = bf16[48,1024]{1,0:T(8,128)(2,1)S(1)} copy-done((bf16[48,1024]{1,0:T(8,128)(2,1)S(1)}, bf16[48,1024]{1,0:T(8,128)(2,1)}, u32[]{:S(2)}) %copy-start.2) | copy-done | bytes 98328
  4.4 69.9 %fused_grads.1 = (f32[1664,1024]{1,0:T(8,128)S(1)}, bf16[48,1664]{1,0:T(8,128)(2,1)S(1)}) custom-call(bf16[48,1664]{1,0:T(8,128)(2,1)S(1)} %copy-done.1, bf16[48,1024]{1,0:T(8,128)(2,1)S(1)} %copy-done.2, bf16[1664,1024]{1,0:T(8,128)(2,1)S(1)} %copy-done), custom_call_target="tpu_custom_call" | custom-call | tf_op jit(solution)/shard_map/fused_grads/pallas_call | solution.py:259
  74.3 2.9 %copy.7 = f32[1664,1024]{1,0:T(8,128)} copy(f32[1664,1024]{1,0:T(8,128)S(1)} %get-tuple-element.2) | data formatting | bytes 13631488
  77.2 0.7 copy.8
Async XLA Ops:
  0.6 2.0 %copy-start = (bf16[1664,1024]{1,0:T(8,128)(2,1)S(1)}, bf16[1664,1024]{1,0:T(8,128)(2,1)}, u32[]{:S(2)}) copy-start(bf16[1664,1024]{1,0:T(8,128)(2,1)} %weight.1) | copy-start | bytes 10223620
  2.6 0.9 %copy-start.1 = (bf16[48,1664]{1,0:T(8,128)(2,1)S(1)}, bf16[48,1664]{1,0:T(8,128)(2,1)}, u32[]{:S(2)}) copy-start(bf16[48,1664]{1,0:T(8,128)(2,1)} %act.1) | copy-start | bytes 479236
  3.5 0.9 %copy-start.2 = (bf16[48,1024]{1,0:T(8,128)(2,1)S(1)}, bf16[48,1024]{1,0:T(8,128)(2,1)}, u32[]{:S(2)}) copy-start(bf16[48,1024]{1,0:T(8,128)(2,1)} %grad.1) | copy-start | bytes 294916

commit v2 on v1

v2 whole, which is shorter than its diff:
```python
import jax
import jax.numpy as jnp
from jax import lax
from jax.experimental import pallas as pl
from jax.experimental.pallas import tpu as pltpu
from jax.sharding import PartitionSpec as P

SEQ = 96
EXAMPLES = 8
MESH = pl.DeviceIdType.MESH

TOK = 48
HID = 1664
FEAT = 1024
TOKENS = 768
LANES = 128
SUB = 16
GROUPS = TOK // SUB
COLS = HID // LANES
TILES = GROUPS * COLS
RATE = 250.0
OFFSET = 125.0

KINDS = []


def kind(name):
    if name not in KINDS:
        KINDS.append(name)
    return KINDS.index(name)


for name in ("gz0", "gz1", "gz2", "gz3", "gy2"):
    kind(name)
for j in range(4):
    for name in ("gyp", "gym", "gyf"):
        kind((name, j))
for j in range(8):
    kind(("gc", j))
for name in ("az", "axp0", "axm0", "ax2", "axp1", "axm1", "axf1"):
    kind(name)
for j in range(8):
    kind(("ac", j))
kind("w")


def kernel(act, grad, weight, fisher, hidden, act_all, grad_all, grad_mate, w_all, w_t, left, raw, part, recv,
           send_sems, recv_sems, part_send, part_recv, local_sems):
    r, c = lax.axis_index("row"), lax.axis_index("col")
    zh, y = r // 4, r % 4
    zl, x, core = c // 8, (c // 2) % 4, c % 2
    chip = c // 2

    def row_at(dzh, dy):
        return ((zh + dzh) % 4) * 4 + (y + dy) % 4

    def col_at(dzl, dx, dcore):
        return ((zl + dzl) % 2) * 8 + ((x + dx) % 4) * 2 + (core + dcore) % 2

    mate = (r, col_at(0, 0, 1))

    barrier = pltpu.get_barrier_semaphore()
    peers = [(row_at(dzh, 0), c) for dzh in (1, 3)] + [(row_at(0, dy), c) for dy in (1, 2, 3)]
    peers += [(r, col_at(dzl, dx, dc)) for dzl in range(2) for dx in range(4) for dc in range(2) if (dzl, dx, dc) != (0, 0, 0)]
    for peer in peers:
        pl.semaphore_signal(barrier, inc=1, device_id=peer, device_id_type=MESH)

    def rows(b):
        return pl.ds(pl.multiple_of(b * TOK, TOK), TOK)

    local = [
        pltpu.make_async_copy(grad, grad_all.at[rows(r)], local_sems.at[0]),
        pltpu.make_async_copy(act, act_all.at[rows(c)], local_sems.at[1]),
        pltpu.make_async_copy(weight, w_all.at[0], local_sems.at[2]),
    ]
    for copy in local:
        copy.start()
    pl.semaphore_wait(barrier, len(peers))

    sent = []

    def send(name, src, dst, to):
        k = kind(name)
        copy = pltpu.make_async_remote_copy(
            src_ref=src, dst_ref=dst, send_sem=send_sems.at[k], recv_sem=recv_sems.at[k],
            device_id=to, device_id_type=MESH,
        )
        copy.start()
        sent.append((name, copy))

    def arrived(name):
        for n, copy in sent:
            if n == name:
                copy.wait_recv()
                return
        raise ValueError(name)

    def send_grad(name, b, to, src=None, columns=None):
        src, dst = grad_all.at[rows(b)] if src is None else src, grad_all.at[rows(b)]
        if columns is not None:
            src, dst = src.at[:, columns], dst.at[:, columns]
        send(name, src, dst, to)

    def send_act(name, b, to, src=None):
        send(name, act_all.at[rows(b)] if src is None else src, act_all.at[rows(b)], to)

    zstep = (0, -1, 1, 2)

    def to_mate(first, y_block):
        for i in range(2):
            b = ((1 - core) + 2 * i) * 4 + y_block
            send(("gc", first + i), grad_all.at[rows(b)], grad_mate.at[rows(b)], mate)

    def turn(half):
        @pl.loop(0, COLS)
        def _(n):
            at = pl.ds(pl.multiple_of(n * LANES, LANES), LANES)
            w_t[pl.ds(half * FEAT, FEAT), at] = w_all[half, at, :].T

    up, down, over = (row_at(0, 1), c), (row_at(0, -1), c), (row_at(0, 2), c)
    right, far = (r, col_at(0, 1, 0)), (r, col_at(0, 2, 0))
    back = (r, col_at(0, -1, 0))

    send_grad("gz0", r, (row_at(1, 0), c), grad)
    send_grad("gz1", r, (row_at(-1, 0), c), grad)
    send_grad(("gyp", 0), r, up, grad)
    send_grad(("gym", 0), r, down, grad)
    send_grad("gy2", r, over, grad)
    send_act("axp0", c, right, act)
    send_act("axm0", c, back, act)
    send("w", weight, w_all.at[1], mate)
    send_act("ax2", c, far, act)
    send_act(("ac", 0), c, mate, act)
    local[2].wait()
    turn(0)

    half = FEAT // 2
    arrived("gz0")
    send_grad("gz2", row_at(-1, 0), (row_at(1, 0), c), columns=pl.ds(0, half))
    arrived("gz1")
    send_grad("gz3", row_at(1, 0), (row_at(-1, 0), c), columns=pl.ds(half, half))
    for j in (1, 2):
        send_grad(("gyp", j), row_at(zstep[j], 0), up)
        send_grad(("gym", j), row_at(zstep[j], 0), down)
    send_act("az", c, (r, col_at(1, 0, 0)), act)
    local[0].wait()
    local[1].wait()
    arrived("gz2")
    arrived("gz3")
    send_grad(("gyp", 3), row_at(2, 0), up)
    send_grad(("gym", 3), row_at(2, 0), down)
    to_mate(0, y)
    arrived("az")
    b = col_at(1, 0, 0)
    send_act("axp1", b, right)
    send_act("axm1", b, back)
    send_act(("ac", 1), b, mate)

    def forward_y(j):
        if j < 2:
            arrived(("gyp", j))
            send_grad(("gyf", j), row_at(zstep[j], -1), up)
        else:
            arrived(("gym", j))
            send_grad(("gyf", j), row_at(zstep[j], 1), down)

    forward_y(1)
    forward_y(2)
    arrived("axp0")
    send_act(("ac", 2), col_at(0, -1, 0), mate)
    arrived("axm0")
    send_act(("ac", 3), col_at(0, 1, 0), mate)
    forward_y(3)
    arrived("ax2")
    send_act(("ac", 6), col_at(0, 2, 0), mate)
    arrived("axm1")
    b = col_at(1, 1, 0)
    send_act("axf1", b, back)
    send_act(("ac", 4), b, mate)
    arrived("w")
    turn(1)

    def multiply(first, y_blocks):
        blocks = [(core + 2 * i) * 4 + yb for yb in y_blocks for i in range(2)]
        count = len(blocks)
        for i, b in enumerate(blocks):
            left[pl.ds(i * TOK, TOK), pl.ds(0, FEAT)] = grad_all[rows(b), :]
            left[pl.ds(i * TOK, TOK), pl.ds(FEAT, FEAT)] = grad_mate[rows(b), :]

        raw[pl.ds(0, count * TOK), :] = jnp.dot(
            left[pl.ds(0, count * TOK), :], w_t[...], preferred_element_type=jnp.float32
        )

        @pl.loop(0, count)
        def _(i):
            lane = lax.broadcasted_iota(jnp.int32, (SUB, LANES), 1)
            scales = jnp.zeros((SUB, LANES), jnp.float32)
            for g in range(GROUPS):
                at = pl.ds(pl.multiple_of(i * TOK + g * SUB, SUB), SUB)
                top = jnp.max(jnp.abs(raw[at, :]), axis=1, keepdims=True)
                top = top.astype(jnp.bfloat16).astype(jnp.float32)
                inverse = jnp.where(top > 0, 1.0 / jnp.where(top > 0, top, 1.0), 0.0)
                scales = jnp.where(lane // 32 == g, top, scales)
                for n in range(COLS):
                    value = raw[at, pl.ds(n * LANES, LANES)]
                    level = jnp.abs(value) * inverse + 1e-30
                    code = jnp.exp2(RATE * level * lax.rsqrt(level) - OFFSET)
                    part[first + i, g * COLS + n] = jnp.where(value < 0, -code, code).astype(jnp.bfloat16)
            part[first + i, TILES] = scales.astype(jnp.bfloat16)

            yb = y_blocks[0] if len(y_blocks) == 1 else jnp.where(i < 2, y_blocks[0], y_blocks[1])
            b = (core + 2 * (i % 2)) * 4 + yb

            @pl.when(b == c)
            def _():
                pltpu.make_async_copy(part.at[first + i], recv.at[chip], part_recv.at[chip]).start()

            @pl.when(b != c)
            def _():
                pltpu.make_async_remote_copy(
                    src_ref=part.at[first + i], dst_ref=recv.at[chip], send_sem=part_send.at[first + i],
                    recv_sem=part_recv.at[chip], device_id=(r, b), device_id_type=MESH,
                ).start()

        return blocks

    arrived(("gc", 0))
    arrived(("gc", 1))
    dests = multiply(0, [y])

    arrived("axp1")
    send_act(("ac", 5), col_at(1, -1, 0), mate)
    for j in (0, 2, 3):
        arrived(("gyp", j))
    to_mate(2, (y - 1) % 4)
    for j in (0, 1):
        arrived(("gym", j))
    to_mate(4, (y + 1) % 4)
    arrived("axf1")
    send_act(("ac", 7), col_at(1, 2, 0), mate)
    for j in range(2, 6):
        arrived(("gc", j))
    dests += multiply(2, [(y - 1) % 4, (y + 1) % 4])

    arrived("gy2")
    for j in range(1, 4):
        arrived(("gyf", j))
    to_mate(6, (y + 2) % 4)
    for j in range(6, 8):
        arrived(("gc", j))
    dests += multiply(6, [(y + 2) % 4])

    for j in range(8):
        arrived(("ac", j))

    def fisher_rows(start, height):
        for f in range(FEAT // 256):
            total = None
            for e in range(EXAMPLES):
                piece = lax.dot_general(
                    act_all[pl.ds(e * SEQ, SEQ), pl.ds(start, height)], grad_all[pl.ds(e * SEQ, SEQ), pl.ds(f * 256, 256)],
                    (((0,), (0,)), ((), ())), preferred_element_type=jnp.float32,
                )
                total = piece * piece if total is None else total + piece * piece
            fisher[pl.ds(start, height), pl.ds(f * 256, 256)] = total * (1.0 / (EXAMPLES * SEQ))

    @pl.loop(0, HID // 512)
    def _(n):
        fisher_rows(pl.multiple_of(n * 512, 512), 512)

    fisher_rows(HID // 512 * 512, HID % 512)

    for k in range(8):
        pltpu.make_async_copy(part.at[0], recv.at[k], part_recv.at[k]).wait()

    for g in range(GROUPS):
        scales = [recv[k, TILES, :, pl.ds(g * 32, 1)].astype(jnp.float32) * (1.0 / RATE ** 2) for k in range(8)]

        for n in range(COLS):
            total = jnp.zeros((SUB, LANES), jnp.float32)
            for k in range(8):
                code = recv[k, g * COLS + n].astype(jnp.float32)
                level = jnp.log2(jnp.abs(code)) + OFFSET
                value = scales[k] * level * level
                total = total + jnp.where(code < 0, -value, value)
            hidden[pl.ds(g * SUB, SUB), pl.ds(n * LANES, LANES)] = total.astype(jnp.bfloat16)

    for _, copy in sent:
        copy.wait_send()
    for i, b in enumerate(dests):
        @pl.when(b != c)
        def _():
            pltpu.make_async_remote_copy(
                src_ref=part.at[i], dst_ref=recv.at[chip], send_sem=part_send.at[i],
                recv_sem=part_recv.at[chip], device_id=(r, b), device_id_type=MESH,
            ).wait_send()


def per_device(hidden_act, out_grad, down_weight):
    any_spec = pl.BlockSpec(memory_space=pl.ANY)
    return pl.pallas_call(
        kernel,
        out_shape=(
            pltpu.VMEM((HID, FEAT), jnp.float32),
            jax.ShapeDtypeStruct((TOK, HID), jnp.bfloat16),
        ),
        in_specs=[any_spec] * 3,
        out_specs=(pl.BlockSpec(memory_space=pltpu.VMEM), pl.BlockSpec(memory_space=pltpu.VMEM)),
        scratch_shapes=[
            pltpu.VMEM((TOKENS, HID), jnp.bfloat16),
            pltpu.VMEM((TOKENS, FEAT), jnp.bfloat16),
            pltpu.VMEM((TOKENS, FEAT), jnp.bfloat16),
            pltpu.VMEM((2, HID, FEAT), jnp.bfloat16),
            pltpu.VMEM((2 * FEAT, HID), jnp.bfloat16),
            pltpu.VMEM((4 * TOK, 2 * FEAT), jnp.bfloat16),
            pltpu.VMEM((4 * TOK, HID), jnp.float32),
            pltpu.VMEM((8, TILES + 1, SUB, LANES), jnp.bfloat16),
            pltpu.VMEM((8, TILES + 1, SUB, LANES), jnp.bfloat16),
            pltpu.SemaphoreType.DMA((len(KINDS),)),
            pltpu.SemaphoreType.DMA((len(KINDS),)),
            pltpu.SemaphoreType.DMA((8,)),
            pltpu.SemaphoreType.DMA((8,)),
            pltpu.SemaphoreType.DMA((3,)),
        ],
        compiler_params=pltpu.CompilerParams(
            collective_id=0, has_side_effects=True, vmem_limit_bytes=60 * 1000 * 1000,
        ),
        name="fused_grads",
    )(hidden_act, out_grad, down_weight)


def solution(mesh):
    placed = (P("col", "row"), P("row", "col"), P("row", "col"))
    return jax.shard_map(
        per_device,
        mesh=mesh,
        in_specs=placed,
        out_specs=(P("row", "col"), P("col", "row")),
        check_vma=False,
    )
```

time: 78 us -> 62.7 us (0.80)
  the two profiles are of different devices: /device:TPU:8 before, /device:TPU:31 now
where the time goes in v2:
time: 62.7 us; the launch traced here: 62.6 us
  Pallas kernels  58.4 us (93%)
  local copies, waits for them, and re-layouts  3.55 us (6%)
  between operations  0.65 us (1%)
    pallas_call x1, Pallas kernels, per_device(): pl.pallas_call(kernel, out_shape=(pltpu.VMEM((HID, FEAT), jnp.float32), j...  58.4 us
    unnamed x4, local copies, waits for them, and re-layouts  3.55 us

profile of v2, /device:TPU:31, one launch (start us, length us, event | category | flops | bytes accessed | tf_op | source)
XLA Modules:
  0.0 62.6 jit_solution(3582959017976502341)
XLA Ops:
  0.6 58.4 %fused_grads.1 = (f32[1664,1024]{1,0:T(8,128)S(1)}, bf16[48,1664]{1,0:T(8,128)(2,1)}) custom-call(bf16[48,1664]{1,0:T(8,128)(2,1)} %act.1, bf16[48,1024]{1,0:T(8,128)(2,1)} %grad.1, bf16[1664,1024]{1,0:T(8,128)(2,1)} %weight.1), custom_call_target="tpu_custom_call" | custom-call | tf_op jit(solution)/shard_map/fused_grads/pallas_call | solution.py:301
  59.0 0.0 copy-start
  59.1 2.9 %copy.7 = f32[1664,1024]{1,0:T(8,128)} copy(f32[1664,1024]{1,0:T(8,128)S(1)} %get-tuple-element.2) | data formatting | bytes 13631488
  61.9 0.0 copy-done
  61.9 0.7 %copy.8 = bf16[48,1664]{1,0:T(8,128)(2,1)} copy(bf16[48,1664]{1,0:T(8,128)(2,1)S(1)} %copy-done) | data formatting | bytes 319488
Async XLA Ops:
  59.0 2.9 %copy-start = (bf16[48,1664]{1,0:T(8,128)(2,1)S(1)}, bf16[48,1664]{1,0:T(8,128)(2,1)}, u32[]{:S(2)}) copy-start(bf16[48,1664]{1,0:T(8,128)(2,1)} %get-tuple-element.7) | copy-start | bytes 479236

commit v3 on v2

--- a/solution.py
+++ b/solution.py
@@ -18,6 +18,7 @@
 GROUPS = TOK // SUB
 COLS = HID // LANES
 TILES = GROUPS * COLS
+CHUNKS = 8
 RATE = 250.0
 OFFSET = 125.0
 
@@ -44,7 +45,7 @@
 kind("w")
 
 
-def kernel(act, grad, weight, fisher, hidden, act_all, grad_all, grad_mate, w_all, w_t, left, raw, part, recv,
+def kernel(act, grad, weight, fisher, recv, act_all, grad_all, grad_mate, w_all, w_t, left, raw, part,
            send_sems, recv_sems, part_send, part_recv, local_sems):
     r, c = lax.axis_index("row"), lax.axis_index("col")
     zh, y = r // 4, r % 4
@@ -120,6 +121,50 @@
     up, down, over = (row_at(0, 1), c), (row_at(0, -1), c), (row_at(0, 2), c)
     right, far = (r, col_at(0, 1, 0)), (r, col_at(0, 2, 0))
     back = (r, col_at(0, -1, 0))
+
+    def multiply(first, y_blocks):
+        blocks = [(core + 2 * i) * 4 + yb for yb in y_blocks for i in range(2)]
+        count = len(blocks)
+        for i, b in enumerate(blocks):
+            left[pl.ds(i * TOK, TOK), pl.ds(0, FEAT)] = grad_all[rows(b), :]
+            left[pl.ds(i * TOK, TOK), pl.ds(FEAT, FEAT)] = grad_mate[rows(b), :]
+
+        raw[pl.ds(0, count * TOK), :] = jnp.dot(
+            left[pl.ds(0, count * TOK), :], w_t[...], preferred_element_type=jnp.float32
+        )
+
+        @pl.loop(0, count)
+        def _(i):
+            lane = lax.broadcasted_iota(jnp.int32, (SUB, LANES), 1)
+            scales = jnp.zeros((SUB, LANES), jnp.float32)
+            for g in range(GROUPS):
+                at = pl.ds(pl.multiple_of(i * TOK + g * SUB, SUB), SUB)
+                top = jnp.max(jnp.abs(raw[at, :]), axis=1, keepdims=True)
+                top = top.astype(jnp.bfloat16).astype(jnp.float32)
+                inverse = jnp.where(top > 0, 1.0 / jnp.where(top > 0, top, 1.0), 0.0)
+                scales = jnp.where(lane // 32 == g, top, scales)
+                for n in range(COLS):
+                    value = raw[at, pl.ds(n * LANES, LANES)]
+                    level = jnp.abs(value) * inverse + 1e-30
+                    code = jnp.exp2(RATE * level * lax.rsqrt(level) - OFFSET)
+                    part[first + i, g * COLS + n] = jnp.where(value < 0, -code, code).astype(jnp.bfloat16)
+            part[first + i, TILES] = scales.astype(jnp.bfloat16)
+
+            yb = y_blocks[0] if len(y_blocks) == 1 else jnp.where(i < 2, y_blocks[0], y_blocks[1])
+            b = (core + 2 * (i % 2)) * 4 + yb
+
+            @pl.when(b == c)
+            def _():
+                pltpu.make_async_copy(part.at[first + i], recv.at[chip], part_recv.at[chip]).start()
+
+            @pl.when(b != c)
+            def _():
+                pltpu.make_async_remote_copy(
+                    src_ref=part.at[first + i], dst_ref=recv.at[chip], send_sem=part_send.at[first + i],
+                    recv_sem=part_recv.at[chip], device_id=(r, b), device_id_type=MESH,
+                ).start()
+
+        return blocks
 
     send_grad("gz0", r, (row_at(1, 0), c), grad)
     send_grad("gz1", r, (row_at(-1, 0), c), grad)
@@ -166,82 +211,37 @@
 
     forward_y(1)
     forward_y(2)
+    arrived("w")
+    turn(1)
+    arrived(("gc", 0))
+    arrived(("gc", 1))
+    dests = multiply(0, [y])
+
+    forward_y(3)
+    for j in (0, 2, 3):
+        arrived(("gyp", j))
+    to_mate(2, (y - 1) % 4)
+    for j in (0, 1):
+        arrived(("gym", j))
+    to_mate(4, (y + 1) % 4)
     arrived("axp0")
     send_act(("ac", 2), col_at(0, -1, 0), mate)
     arrived("axm0")
     send_act(("ac", 3), col_at(0, 1, 0), mate)
-    forward_y(3)
     arrived("ax2")
     send_act(("ac", 6), col_at(0, 2, 0), mate)
     arrived("axm1")
     b = col_at(1, 1, 0)
     send_act("axf1", b, back)
     send_act(("ac", 4), b, mate)
-    arrived("w")
-    turn(1)
-
-    def multiply(first, y_blocks):
-        blocks = [(core + 2 * i) * 4 + yb for yb in y_blocks for i in range(2)]
-        count = len(blocks)
-        for i, b in enumerate(blocks):
-            left[pl.ds(i * TOK, TOK), pl.ds(0, FEAT)] = grad_all[rows(b), :]
-            left[pl.ds(i * TOK, TOK), pl.ds(FEAT, FEAT)] = grad_mate[rows(b), :]
-
-        raw[pl.ds(0, count * TOK), :] = jnp.dot(
-            left[pl.ds(0, count * TOK), :], w_t[...], preferred_element_type=jnp.float32
-        )
-
-        @pl.loop(0, count)
-        def _(i):
-            lane = lax.broadcasted_iota(jnp.int32, (SUB, LANES), 1)
-            scales = jnp.zeros((SUB, LANES), jnp.float32)
-            for g in range(GROUPS):
-                at = pl.ds(pl.multiple_of(i * TOK + g * SUB, SUB), SUB)
-                top = jnp.max(jnp.abs(raw[at, :]), axis=1, keepdims=True)
-                top = top.astype(jnp.bfloat16).astype(jnp.float32)
-                inverse = jnp.where(top > 0, 1.0 / jnp.where(top > 0, top, 1.0), 0.0)
-                scales = jnp.where(lane // 32 == g, top, scales)
-                for n in range(COLS):
-                    value = raw[at, pl.ds(n * LANES, LANES)]
-                    level = jnp.abs(value) * inverse + 1e-30
-                    code = jnp.exp2(RATE * level * lax.rsqrt(level) - OFFSET)
-                    part[first + i, g * COLS + n] = jnp.where(value < 0, -code, code).astype(jnp.bfloat16)
-            part[first + i, TILES] = scales.astype(jnp.bfloat16)
-
-            yb = y_blocks[0] if len(y_blocks) == 1 else jnp.where(i < 2, y_blocks[0], y_blocks[1])
-            b = (core + 2 * (i % 2)) * 4 + yb
-
-            @pl.when(b == c)
-            def _():
-                pltpu.make_async_copy(part.at[first + i], recv.at[chip], part_recv.at[chip]).start()
-
-            @pl.when(b != c)
-            def _():
-                pltpu.make_async_remote_copy(
-                    src_ref=part.at[first + i], dst_ref=recv.at[chip], send_sem=part_send.at[first + i],
-                    recv_sem=part_recv.at[chip], device_id=(r, b), device_id_type=MESH,
-                ).start()
-
-        return blocks
-
-    arrived(("gc", 0))
-    arrived(("gc", 1))
-    dests = multiply(0, [y])
-
-    arrived("axp1")
-    send_act(("ac", 5), col_at(1, -1, 0), mate)
-    for j in (0, 2, 3):
-        arrived(("gyp", j))
-    to_mate(2, (y - 1) % 4)
-    for j in (0, 1):
-        arrived(("gym", j))
-    to_mate(4, (y + 1) % 4)
-    arrived("axf1")
-    send_act(("ac", 7), col_at(1, 2, 0), mate)
     for j in range(2, 6):
         arrived(("gc", j))
     dests += multiply(2, [(y - 1) % 4, (y + 1) % 4])
 
+    arrived("axp1")
+    send_act(("ac", 5), col_at(1, -1, 0), mate)
+    arrived("axf1")
+    send_act(("ac", 7), col_at(1, 2, 0), mate)
     arrived("gy2")
     for j in range(1, 4):
         arrived(("gyf", j))
@@ -273,18 +273,6 @@
     for k in range(8):
         pltpu.make_async_copy(part.at[0], recv.at[k], part_recv.at[k]).wait()
 
-    for g in range(GROUPS):
-        scales = [recv[k, TILES, :, pl.ds(g * 32, 1)].astype(jnp.float32) * (1.0 / RATE ** 2) for k in range(8)]
-
-        for n in range(COLS):
-            total = jnp.zeros((SUB, LANES), jnp.float32)
-            for k in range(8):
-                code = recv[k, g * COLS + n].astype(jnp.float32)
-                level = jnp.log2(jnp.abs(code)) + OFFSET
-                value = scales[k] * level * level
-                total = total + jnp.where(code < 0, -value, value)
-            hidden[pl.ds(g * SUB, SUB), pl.ds(n * LANES, LANES)] = total.astype(jnp.bfloat16)
-
     for _, copy in sent:
         copy.wait_send()
     for i, b in enumerate(dests):
@@ -296,13 +284,40 @@
             ).wait_send()
 
 
+def finish(fisher, recv, fisher_out, hidden_out, hidden, sems):
+    height = HID // CHUNKS
+    copies = [
+        pltpu.make_async_copy(fisher.at[pl.ds(i * height, height)], fisher_out.at[pl.ds(i * height, height)], sems.at[i])
+        for i in range(CHUNKS)
+    ]
+    for copy in copies:
+        copy.start()
+    for g in range(GROUPS):
+        scales = [recv[k, TILES, :, pl.ds(g * 32, 1)].astype(jnp.float32) * (1.0 / RATE ** 2) for k in range(8)]
+
+        for n in range(COLS):
+            total = jnp.zeros((SUB, LANES), jnp.float32)
+            for k in range(8):
+                code = recv[k, g * COLS + n].astype(jnp.float32)
+                level = jnp.log2(jnp.abs(code)) + OFFSET
+                value = scales[k] * level * level
+                total = total + jnp.where(code < 0, -value, value)
+            hidden[pl.ds(g * SUB, SUB), pl.ds(n * LANES, LANES)] = total.astype(jnp.bfloat16)
+
+    last = pltpu.make_async_copy(hidden, hidden_out, sems.at[CHUNKS])
+    last.start()
+    for copy in copies:
+        copy.wait()
+    last.wait()
+
+
 def per_device(hidden_act, out_grad, down_weight):
     any_spec = pl.BlockSpec(memory_space=pl.ANY)
-    return pl.pallas_call(
+    fisher, recv = pl.pallas_call(
         kernel,
         out_shape=(
             pltpu.VMEM((HID, FEAT), jnp.float32),
-            jax.ShapeDtypeStruct((TOK, HID), jnp.bfloat16),
+            pltpu.VMEM((8, TILES + 1, SUB, LANES), jnp.bfloat16),
         ),
         in_specs=[any_spec] * 3,
         out_specs=(pl.BlockSpec(memory_space=pltpu.VMEM), pl.BlockSpec(memory_space=pltpu.VMEM)),
@@ -315,7 +330,6 @@
             pltpu.VMEM((4 * TOK, 2 * FEAT), jnp.bfloat16),
             pltpu.VMEM((4 * TOK, HID), jnp.float32),
             pltpu.VMEM((8, TILES + 1, SUB, LANES), jnp.bfloat16),
-            pltpu.VMEM((8, TILES + 1, SUB, LANES), jnp.bfloat16),
             pltpu.SemaphoreType.DMA((len(KINDS),)),
             pltpu.SemaphoreType.DMA((len(KINDS),)),
             pltpu.SemaphoreType.DMA((8,)),
@@ -323,10 +337,22 @@
             pltpu.SemaphoreType.DMA((3,)),
         ],
         compiler_params=pltpu.CompilerParams(
-            collective_id=0, has_side_effects=True, vmem_limit_bytes=60 * 1000 * 1000,
+            collective_id=0, has_side_effects=True, vmem_limit_bytes=58300 * 1000,
         ),
         name="fused_grads",
     )(hidden_act, out_grad, down_weight)
+    return pl.pallas_call(
+        finish,
+        out_shape=(
+            jax.ShapeDtypeStruct((HID, FEAT), jnp.float32),
+            jax.ShapeDtypeStruct((TOK, HID), jnp.bfloat16),
+        ),
+        in_specs=[any_spec, pl.BlockSpec(memory_space=pltpu.VMEM)],
+        out_specs=(any_spec, any_spec),
+        scratch_shapes=[pltpu.VMEM((TOK, HID), jnp.bfloat16), pltpu.SemaphoreType.DMA((CHUNKS + 1,))],
+        compiler_params=pltpu.CompilerParams(vmem_limit_bytes=40 * 1000 * 1000),
+        name="write_out",
+    )(fisher, recv)
 
 
 def solution(mesh):

time: 62.7 us -> 58.2 us (0.928)
  local copies, waits for them, and re-layouts: 3.55 us -> 0 us
  Pallas kernels: 58.4 us -> 57.5 us
    unnamed x4 -> x0, local copies, waits for them, and re-layouts: 3.55 us -> none
    pallas_call x1 -> x2, Pallas kernels: 58.4 us -> 57.5 us  [the longest x1 54.5 us: per_device(): pl.pallas_call(kernel, out_shape=(pltpu.VMEM((HID, FEAT), jnp.float32), p...]
where the time goes in v3:
time: 58.2 us; the launch traced here: 58.1 us
  Pallas kernels  57.5 us (99%)
  between operations  0.64 us (1%)
    pallas_call x1, Pallas kernels, per_device(): pl.pallas_call(kernel, out_shape=(pltpu.VMEM((HID, FEAT), jnp.float32), p...  54.5 us
    pallas_call x1, Pallas kernels, per_device(): pl.pallas_call(finish, out_shape=(jax.ShapeDtypeStruct((HID, FEAT), jnp.f...  2.92 us

profile of v3, /device:TPU:31, one launch (start us, length us, event | category | flops | bytes accessed | tf_op | source)
XLA Modules:
  0.0 58.1 jit_solution(7250624152989202649)
XLA Ops:
  0.6 54.5 %fused_grads.1 = (f32[1664,1024]{1,0:T(8,128)S(1)}, bf16[8,40,16,128]{3,2,1,0:T(8,128)(2,1)S(1)}) custom-call(bf16[48,1664]{1,0:T(8,128)(2,1)} %act.1, bf16[48,1024]{1,0:T(8,128)(2,1)} %grad.1, bf16[1664,1024]{1,0:T(8,128)(2,1)} %weight.1), custom_call_target="tpu_custom_call" | custom-call | tf_op jit(solution)/shard_map/fused_grads/pallas_call | solution.py:316
  55.2 2.9 %write_out.1 = (f32[1664,1024]{1,0:T(8,128)}, bf16[48,1664]{1,0:T(8,128)(2,1)}) custom-call(f32[1664,1024]{1,0:T(8,128)S(1)} %get-tuple-element.4.fisher, bf16[8,40,16,128]{3,2,1,0:T(8,128)(2,1)S(1)} %get-tuple-element.5.recv), custom_call_target="tpu_custom_call" | custom-call | tf_op jit(solution)/shard_map/write_out/pallas_call | solution.py:344

commit v4 on v3

--- a/solution.py
+++ b/solution.py
@@ -230,18 +230,14 @@
     send_act(("ac", 3), col_at(0, 1, 0), mate)
     arrived("ax2")
     send_act(("ac", 6), col_at(0, 2, 0), mate)
+    for j in range(2, 6):
+        arrived(("gc", j))
+    dests += multiply(2, [(y - 1) % 4, (y + 1) % 4])
+
     arrived("axm1")
     b = col_at(1, 1, 0)
     send_act("axf1", b, back)
     send_act(("ac", 4), b, mate)
-    for j in range(2, 6):
-        arrived(("gc", j))
-    dests += multiply(2, [(y - 1) % 4, (y + 1) % 4])
-
-    arrived("axp1")
-    send_act(("ac", 5), col_at(1, -1, 0), mate)
-    arrived("axf1")
-    send_act(("ac", 7), col_at(1, 2, 0), mate)
     arrived("gy2")
     for j in range(1, 4):
         arrived(("gyf", j))
@@ -250,25 +246,41 @@
         arrived(("gc", j))
     dests += multiply(6, [(y + 2) % 4])
 
-    for j in range(8):
-        arrived(("ac", j))
-
-    def fisher_rows(start, height):
+    early = [zl * 4 + e for e in range(4)] + [col_at(1, 0, 0) // 2, col_at(1, 1, 0) // 2]
+    late = [col_at(1, 2, 0) // 2, col_at(1, 3, 0) // 2]
+
+    def fisher_rows(start, height, examples, is_last):
         for f in range(FEAT // 256):
-            total = None
-            for e in range(EXAMPLES):
+            at = pl.ds(start, height), pl.ds(f * 256, 256)
+            total = fisher[at] if is_last else None
+            for e in examples:
+                tokens = pl.ds(pl.multiple_of(e * SEQ, SEQ), SEQ)
                 piece = lax.dot_general(
-                    act_all[pl.ds(e * SEQ, SEQ), pl.ds(start, height)], grad_all[pl.ds(e * SEQ, SEQ), pl.ds(f * 256, 256)],
+                    act_all[tokens, pl.ds(start, height)], grad_all[tokens, pl.ds(f * 256, 256)],
                     (((0,), (0,)), ((), ())), preferred_element_type=jnp.float32,
                 )
                 total = piece * piece if total is None else total + piece * piece
-            fisher[pl.ds(start, height), pl.ds(f * 256, 256)] = total * (1.0 / (EXAMPLES * SEQ))
+            fisher[at] = total * (1.0 / (EXAMPLES * SEQ)) if is_last else total
+
+    for j in (0, 1, 2, 3, 4, 6):
+        arrived(("ac", j))
+
+    fisher_rows(0, 512, early, False)
+    arrived("axp1")
+    send_act(("ac", 5), col_at(1, -1, 0), mate)
+    fisher_rows(512, 512, early, False)
+    arrived("axf1")
+    send_act(("ac", 7), col_at(1, 2, 0), mate)
+    fisher_rows(1024, 512, early, False)
+    fisher_rows(1536, 128, early, False)
+    for j in (5, 7):
+        arrived(("ac", j))
 
     @pl.loop(0, HID // 512)
     def _(n):
-        fisher_rows(pl.multiple_of(n * 512, 512), 512)
-
-    fisher_rows(HID // 512 * 512, HID % 512)
+        fisher_rows(pl.multiple_of(n * 512, 512), 512, late, True)
+
+    fisher_rows(1536, 128, late, True)
 
     for k in range(8):
         pltpu.make_async_copy(part.at[0], recv.at[k], part_recv.at[k]).wait()

time: 58.2 us -> 56.4 us (0.969)
  the two profiles are of different devices: /device:TPU:31 before, /device:TPU:15 now
where the time goes in v4:
time: 56.4 us; the launch traced here: 56.3 us
  Pallas kernels  55.7 us (99%)
  between operations  0.64 us (1%)
    pallas_call x1, Pallas kernels, per_device(): pl.pallas_call(kernel, out_shape=(pltpu.VMEM((HID, FEAT), jnp.float32), p...  52.8 us
    pallas_call x1, Pallas kernels, per_device(): pl.pallas_call(finish, out_shape=(jax.ShapeDtypeStruct((HID, FEAT), jnp.f...  2.92 us

profile of v4, /device:TPU:15, one launch (start us, length us, event | category | flops | bytes accessed | tf_op | source)
XLA Modules:
  0.0 56.3 jit_solution(1768429146326490689)
XLA Ops:
  0.6 52.8 %fused_grads.1 = (f32[1664,1024]{1,0:T(8,128)S(1)}, bf16[8,40,16,128]{3,2,1,0:T(8,128)(2,1)S(1)}) custom-call(bf16[48,1664]{1,0:T(8,128)(2,1)} %act.1, bf16[48,1024]{1,0:T(8,128)(2,1)} %grad.1, bf16[1664,1024]{1,0:T(8,128)(2,1)} %weight.1), custom_call_target="tpu_custom_call" | custom-call | tf_op jit(solution)/shard_map/fused_grads/pallas_call | solution.py:328
  53.4 2.9 %write_out.1 = (f32[1664,1024]{1,0:T(8,128)}, bf16[48,1664]{1,0:T(8,128)(2,1)}) custom-call(f32[1664,1024]{1,0:T(8,128)S(1)} %get-tuple-element.4.fisher, bf16[8,40,16,128]{3,2,1,0:T(8,128)(2,1)S(1)} %get-tuple-element.5.recv), custom_call_target="tpu_custom_call" | custom-call | tf_op jit(solution)/shard_map/write_out/pallas_call | solution.py:356

commit v5 on v4

--- a/solution.py
+++ b/solution.py
@@ -230,14 +230,14 @@
     send_act(("ac", 3), col_at(0, 1, 0), mate)
     arrived("ax2")
     send_act(("ac", 6), col_at(0, 2, 0), mate)
-    for j in range(2, 6):
-        arrived(("gc", j))
-    dests += multiply(2, [(y - 1) % 4, (y + 1) % 4])
-
     arrived("axm1")
     b = col_at(1, 1, 0)
     send_act("axf1", b, back)
     send_act(("ac", 4), b, mate)
+    for j in range(2, 6):
+        arrived(("gc", j))
+    dests += multiply(2, [(y - 1) % 4, (y + 1) % 4])
+
     arrived("gy2")
     for j in range(1, 4):
         arrived(("gyf", j))

time: 56.4 us -> 56 us (level)
  the two profiles are of different devices: /device:TPU:15 before, /device:TPU:31 now
where the time goes in v5:
time: 56 us; the launch traced here: 55.9 us
  Pallas kernels  55.3 us (99%)
  between operations  0.64 us (1%)
    pallas_call x1, Pallas kernels, per_device(): pl.pallas_call(kernel, out_shape=(pltpu.VMEM((HID, FEAT), jnp.float32), p...  52.4 us
    pallas_call x1, Pallas kernels, per_device(): pl.pallas_call(finish, out_shape=(jax.ShapeDtypeStruct((HID, FEAT), jnp.f...  2.92 us

profile of v5, /device:TPU:31, one launch (start us, length us, event | category | flops | bytes accessed | tf_op | source)
XLA Modules:
  0.0 55.9 jit_solution(2180527987595945081)
XLA Ops:
  0.6 52.4 %fused_grads.1 = (f32[1664,1024]{1,0:T(8,128)S(1)}, bf16[8,40,16,128]{3,2,1,0:T(8,128)(2,1)S(1)}) custom-call(bf16[48,1664]{1,0:T(8,128)(2,1)} %act.1, bf16[48,1024]{1,0:T(8,128)(2,1)} %grad.1, bf16[1664,1024]{1,0:T(8,128)(2,1)} %weight.1), custom_call_target="tpu_custom_call" | custom-call | tf_op jit(solution)/shard_map/fused_grads/pallas_call | solution.py:328
  53.0 2.9 %write_out.1 = (f32[1664,1024]{1,0:T(8,128)}, bf16[48,1664]{1,0:T(8,128)(2,1)}) custom-call(f32[1664,1024]{1,0:T(8,128)S(1)} %get-tuple-element.4.fisher, bf16[8,40,16,128]{3,2,1,0:T(8,128)(2,1)S(1)} %get-tuple-element.5.recv), custom_call_target="tpu_custom_call" | custom-call | tf_op jit(solution)/shard_map/write_out/pallas_call | solution.py:356

commit v6 on v5

--- a/solution.py
+++ b/solution.py
@@ -150,8 +150,7 @@
                     part[first + i, g * COLS + n] = jnp.where(value < 0, -code, code).astype(jnp.bfloat16)
             part[first + i, TILES] = scales.astype(jnp.bfloat16)
 
-            yb = y_blocks[0] if len(y_blocks) == 1 else jnp.where(i < 2, y_blocks[0], y_blocks[1])
-            b = (core + 2 * (i % 2)) * 4 + yb
+            b = (core + 2 * i) * 4 + y_blocks[0]
 
             @pl.when(b == c)
             def _():
@@ -234,9 +233,12 @@
     b = col_at(1, 1, 0)
     send_act("axf1", b, back)
     send_act(("ac", 4), b, mate)
-    for j in range(2, 6):
+    for j in (2, 3):
         arrived(("gc", j))
-    dests += multiply(2, [(y - 1) % 4, (y + 1) % 4])
+    dests += multiply(2, [(y - 1) % 4])
+    for j in (4, 5):
+        arrived(("gc", j))
+    dests += multiply(4, [(y + 1) % 4])
 
     arrived("gy2")
     for j in range(1, 4):

time: 56 us -> 56.9 us (1.016)
  Pallas kernels: 55.3 us -> 56.2 us
    pallas_call x1, Pallas kernels: 52.4 us -> 53.2 us  [per_device(): pl.pallas_call(kernel, out_shape=(pltpu.VMEM((HID, FEAT), jnp.float32), p...]
where the time goes in v6:
time: 56.9 us; the launch traced here: 56.8 us
  Pallas kernels  56.2 us (99%)
  between operations  0.64 us (1%)
    pallas_call x1, Pallas kernels, per_device(): pl.pallas_call(kernel, out_shape=(pltpu.VMEM((HID, FEAT), jnp.float32), p...  53.2 us
    pallas_call x1, Pallas kernels, per_device(): pl.pallas_call(finish, out_shape=(jax.ShapeDtypeStruct((HID, FEAT), jnp.f...  2.92 us

profile of v6, /device:TPU:31, one launch (start us, length us, event | category | flops | bytes accessed | tf_op | source)
XLA Modules:
  0.0 56.8 jit_solution(16854736448282269394)
XLA Ops:
  0.6 53.2 %fused_grads.1 = (f32[1664,1024]{1,0:T(8,128)S(1)}, bf16[8,40,16,128]{3,2,1,0:T(8,128)(2,1)S(1)}) custom-call(bf16[48,1664]{1,0:T(8,128)(2,1)} %act.1, bf16[48,1024]{1,0:T(8,128)(2,1)} %grad.1, bf16[1664,1024]{1,0:T(8,128)(2,1)} %weight.1), custom_call_target="tpu_custom_call" | custom-call | tf_op jit(solution)/shard_map/fused_grads/pallas_call | solution.py:330
  53.9 2.9 %write_out.1 = (f32[1664,1024]{1,0:T(8,128)}, bf16[48,1664]{1,0:T(8,128)(2,1)}) custom-call(f32[1664,1024]{1,0:T(8,128)S(1)} %get-tuple-element.4.fisher, bf16[8,40,16,128]{3,2,1,0:T(8,128)(2,1)S(1)} %get-tuple-element.5.recv), custom_call_target="tpu_custom_call" | custom-call | tf_op jit(solution)/shard_map/write_out/pallas_call | solution.py:358
